TPU v7x, 256 devices: a whole 4x4x8 slice. The times are simulated.
256 devices in a mesh: section: 32 (over x, z_lo, core), dp: 8 (over z_hi, y).
Axes of the slice: x: 4, y: 4, z: 8 (z_hi: 2, z_lo: 4; z = z_hi * 4 + z_lo), core: 2. Of those that a mesh axis runs over, the one named last changes fastest.
Arguments:
- inputs: bfloat16 [4, 256, 2560], P(None, 'dp'), may hold values from -6 to 6
- cotangent: bfloat16 [4, 256, 2560], P(None, 'dp'), may hold values from -6 to 6
- weight: bfloat16 [32, 2560, 2560], P('section', 'dp'), may hold values from -5 to 5
- a_inv: bfloat16 [32, 40, 64, 64], P('section', 'dp'), may hold values from -0.15 to 2, as said below
- g_inv: bfloat16 [32, 40, 64, 64], P('section'), may hold values from -0.15 to 2, as said below
Outputs:
- new_weight: bfloat16 [32, 2560, 2560], P('section', 'dp')
- a_fac: float32 [32, 40, 64, 64], P('section')
- g_fac: float32 [32, 40, 64, 64], P('section')
Inputs may be any that keep to these rules, and one draw needn't show every extreme that they name: `a_inv`: blocks of the previous step's inverse factors: positive diagonal, off-diagonal entries small but independent. `g_inv`: blocks of the previous step's inverse factors: positive diagonal, off-diagonal entries small but independent.
All inputs are finite; a program needn't handle non-finite values.
Results may differ from a plain program's by a relative error of at most 0.017.
Values may be sent and summed in bfloat16 or wider, within the bound.
A program may use at most 64 MiB of HBM per device.

v0:
```python
import math

import jax
import jax.numpy as jnp
from jax import lax
from jax.sharding import PartitionSpec as P


def from_behind(value, axis, by):
    size = lax.axis_size(axis)
    pairs = [(i, i + by) for i in range(size) if 0 <= i + by < size]
    return lax.ppermute(value, axis, pairs)


def local(inputs, cotangent, weight, a_inv, g_inv):
    sections = lax.axis_size("section")
    groups = lax.axis_size("dp")
    my_section = lax.axis_index("section")
    micro_count, row_count, features = inputs.shape
    block_size = a_inv.shape[-1]
    n_blocks = g_inv.shape[1]
    local_rows = weight.shape[1]
    token_total = micro_count * row_count * groups
    layer_scale = 0.25 / math.sqrt(features)
    gathered = lax.all_gather(weight, "dp", axis=1, tiled=True)[0]

    def forward_layer(values):
        product = jnp.dot(values, gathered, preferred_element_type=jnp.float32)
        return (values.astype(jnp.float32) + layer_scale * product).astype(jnp.bfloat16)

    def backward_layer(values):
        product = lax.dot_general(
            values, gathered, (((1,), (1,)), ((), ())), preferred_element_type=jnp.float32
        )
        return (values.astype(jnp.float32) + layer_scale * product).astype(jnp.bfloat16)

    def keep_rows(values):
        return values

    zero_rows = jnp.zeros((row_count, features), jnp.bfloat16)
    empty_store = jnp.zeros((micro_count, row_count, features), jnp.bfloat16)
    tick_count = micro_count + sections - 1

    def forward_work(step_index, arrived, kept_rows):
        position = step_index - my_section
        in_use = (position >= 0) & (position < micro_count)
        micro_slot = jnp.clip(position, 0, micro_count - 1)
        incoming = lax.dynamic_index_in_dim(inputs, micro_slot, 0, keepdims=False)
        entering = jnp.where(my_section == 0, incoming, arrived)
        outcome = lax.cond(in_use, forward_layer, keep_rows, entering)
        previous = lax.dynamic_index_in_dim(kept_rows, micro_slot, 0, keepdims=False)
        kept_rows = lax.dynamic_update_index_in_dim(
            kept_rows, jnp.where(in_use, entering, previous), micro_slot, 0
        )
        return (outcome, kept_rows)

    def backward_work(step_index, arrived, kept_rows):
        position = step_index - (sections - 1 - my_section)
        in_use = (position >= 0) & (position < micro_count)
        micro_slot = jnp.clip(position, 0, micro_count - 1)
        incoming = lax.dynamic_index_in_dim(cotangent, micro_slot, 0, keepdims=False)
        entering = jnp.where(my_section == sections - 1, incoming, arrived)
        outcome = lax.cond(in_use, backward_layer, keep_rows, entering)
        previous = lax.dynamic_index_in_dim(kept_rows, micro_slot, 0, keepdims=False)
        kept_rows = lax.dynamic_update_index_in_dim(
            kept_rows, jnp.where(in_use, entering, previous), micro_slot, 0
        )
        return (outcome, kept_rows)

    def joint_tick(step_index, running):
        forward_out, forward_kept, backward_out, backward_kept = running
        forward_in = from_behind(forward_out, "section", 1)
        backward_in = from_behind(backward_out, "section", -1)
        forward_out, forward_kept = forward_work(step_index, forward_in, forward_kept)
        backward_out, backward_kept = backward_work(step_index, backward_in, backward_kept)
        return (forward_out, forward_kept, backward_out, backward_kept)

    _, inputs_saved, _, cotangents_saved = lax.fori_loop(
        0, tick_count, joint_tick, (zero_rows, empty_store, zero_rows, empty_store)
    )
    flat_inputs = inputs_saved.reshape(micro_count * row_count, features)
    flat_cotangents = cotangents_saved.reshape(micro_count * row_count, features)

    def factor_blocks(values):
        grouped = values.reshape(-1, n_blocks, block_size)
        return jnp.einsum("rnb,rnc->nbc", grouped, grouped, preferred_element_type=jnp.float32)

    a_local = factor_blocks(flat_inputs)
    g_local = factor_blocks(flat_cotangents)
    a_summed, g_summed = (
        lax.psum(a_local.astype(jnp.bfloat16), "dp").astype(jnp.float32),
        lax.psum(g_local.astype(jnp.bfloat16), "dp").astype(jnp.float32),
    )
    columns = lax.all_to_all(flat_inputs, "dp", split_axis=1, concat_axis=0, tiled=True)
    every_row = lax.all_gather(flat_cotangents, "dp", axis=0, tiled=True)
    gradient = lax.dot_general(
        columns, every_row, (((0,), (0,)), ((), ())), preferred_element_type=jnp.float32
    )
    gradient = gradient / token_total
    reshaped = gradient.reshape(local_rows // block_size, block_size, n_blocks, block_size)
    left_side = jnp.einsum(
        "bij,bjnk->bink", a_inv[0].astype(jnp.float32), reshaped, precision=lax.Precision.HIGHEST
    )
    precond = jnp.einsum(
        "bink,nkl->binl", left_side, g_inv[0].astype(jnp.float32), precision=lax.Precision.HIGHEST
    )
    updated = (weight[0].astype(jnp.float32) - precond.reshape(local_rows, features)).astype(
        jnp.bfloat16
    )
    return (updated[None], (a_summed / token_total)[None], (g_summed / token_total)[None])


def solution(mesh):
    placed = (
        P(None, "dp", None),
        P(None, "dp", None),
        P("section", "dp", None),
        P("section", "dp", None, None),
        P("section", None, None, None),
    )
    return jax.shard_map(
        local,
        mesh=mesh,
        in_specs=placed,
        out_specs=(
            P("section", "dp", None),
            P("section", None, None, None),
            P("section", None, None, None),
        ),
        check_vma=False,
    )
```

profile of v0, /device:TPU:1, one launch (start us, length us, event | category | flops | bytes accessed | tf_op | source)
XLA Modules:
  0.0 1232.4 jit_solution(18616491608732650)
XLA Ops:
  8.0 255.0 %all-gather.3.cloned.1.call-done = bf16[1,2560,2560]{2,1,0:T(8,128)(2,1)} async-done(((bf16[1,320,2560]{2,1,0:T(8,128)(2,1)}), bf16[1,2560,2560]{2,1,0:T(8,128)(2,1)}) %all-gather.3.cloned.1.call-update) | async-done | bytes 13107216 | tf_op jit(solution)/shard_map/all_gather | solution.py:25
  263.1 643.0 %while.20 = (s32[]{:T(128)}, bf16[32,2560]{1,0:T(8,128)(2,1)S(1)}, bf16[4,32,2560]{2,1,0:T(8,128)(2,1)S(1)}, bf16[32,2560]{1,0:T(8,128)(2,1)S(1)}, bf16[4,32,256...) while((s32[]{:T(128)}, bf16[32,2560]{1,0:T(8,128)(2,1)S(1)}, ...), condition=%wide.region_5.6_spmd, body=%wide.region_0.5_spmd.sunk | while | flops 839843840 | bytes 31130020 | solution.py:78
  273.0 7.6 collective-permute-start.1
  286.8 7.1 conditional.4
  286.8 7.1 fusion.1
  303.7 7.1 conditional.4
  303.8 7.1 fusion.1
  321.4 7.1 conditional.4
  321.5 7.1 fusion.1
  339.1 7.1 conditional.4
  339.2 7.1 fusion.1
  358.8 11.5 collective-permute-start
  387.1 5.8 collective-permute-start
  409.7 11.5 collective-permute-start
  438.0 5.8 collective-permute-start
  460.6 11.5 collective-permute-start
  488.9 13.7 %collective-permute-start = (bf16[32,2560]{1,0:T(8,128)(2,1)S(1)}, bf16[32,2560]{1,0:T(8,128)(2,1)S(1)}, u32[]{:S(2)}, u32[]{:S(2)}) collective-permute-start(bf16[32,2560]{1,0:T(8,128)(2,1)S(1)} %get-tuple-element.373), channel_id=1, source_target_pairs={{0,8},{8,16},{16,24},{24,32},{32,40},{40,48},{48,56},{56,64},{64,7... | collective-permute-start | bytes 491528 | tf_op jit(solution)/shard_map/while/body/eval_jaxpr/ppermute | solution.py:12
  508.8 8.4 collective-permute-start
  523.5 14.2 %collective-permute-start = (bf16[32,2560]{1,0:T(8,128)(2,1)S(1)}, bf16[32,2560]{1,0:T(8,128)(2,1)S(1)}, u32[]{:S(2)}, u32[]{:S(2)}) collective-permute-start(bf16[32,2560]{1,0:T(8,128)(2,1)S(1)} %get-tuple-element.373), channel_id=1, source_target_pairs={{0,8},{8,16},{16,24},{24,32},{32,40},{40,48},{48,56},{56,64},{64,7... | collective-permute-start | bytes 491528 | tf_op jit(solution)/shard_map/while/body/eval_jaxpr/ppermute | solution.py:12
  543.9 8.4 collective-permute-start
  558.5 8.4 collective-permute-start
  573.1 8.4 collective-permute-start
  587.8 8.4 collective-permute-start
  602.5 8.4 collective-permute-start
  617.1 8.4 collective-permute-start
  631.8 8.4 collective-permute-start
  646.4 8.4 collective-permute-start
  661.1 8.4 collective-permute-start
  675.7 8.4 collective-permute-start
  690.4 8.4 collective-permute-start
  705.1 105.2 %collective-permute-start = (bf16[32,2560]{1,0:T(8,128)(2,1)S(1)}, bf16[32,2560]{1,0:T(8,128)(2,1)S(1)}, u32[]{:S(2)}, u32[]{:S(2)}) collective-permute-start(bf16[32,2560]{1,0:T(8,128)(2,1)S(1)} %get-tuple-element.373), channel_id=1, source_target_pairs={{0,8},{8,16},{16,24},{24,32},{32,40},{40,48},{48,56},{56,64},{64,7... | collective-permute-start | bytes 491528 | tf_op jit(solution)/shard_map/while/body/eval_jaxpr/ppermute | solution.py:12
  814.5 8.7 conditional.5
  814.5 8.6 fusion.3
  825.1 8.9 collective-permute-start
  838.2 8.7 conditional.5
  838.3 8.6 fusion.3
  848.9 12.5 %collective-permute-start = (bf16[32,2560]{1,0:T(8,128)(2,1)S(1)}, bf16[32,2560]{1,0:T(8,128)(2,1)S(1)}, u32[]{:S(2)}, u32[]{:S(2)}) collective-permute-start(bf16[32,2560]{1,0:T(8,128)(2,1)S(1)} %get-tuple-element.373), channel_id=1, source_target_pairs={{0,8},{8,16},{16,24},{24,32},{32,40},{40,48},{48,56},{56,64},{64,7... | collective-permute-start | bytes 491528 | tf_op jit(solution)/shard_map/while/body/eval_jaxpr/ppermute | solution.py:12
  865.6 8.7 conditional.5
  865.6 8.6 fusion.3
  876.2 7.1 collective-permute-start
  887.5 8.7 conditional.5
  887.6 8.6 fusion.3
  922.1 134.0 %all-reduce.3.cloned.1.call-done = (bf16[40,64,64]{2,1,0:T(8,128)(2,1)}, bf16[40,64,64]{2,1,0:T(8,128)(2,1)}) async-done(((bf16[40,64,64]{2,1,0:T(8,128)(2,1)}, bf16[40,64,64]{2,1,0:T(8,128)(2,1)}), (bf16[40,64,64]{2,1,0:T(8,128)(2,1)}, bf16[40,64,64]{2,1,0:T(8,128)(2,1)})) %all-reduce.3.cloned.1.call-update) | async-done | bytes 655376 | tf_op jit(solution)/shard_map/psum | solution.py:91
  1059.3 124.4 %all-gather.5.cloned.1.call-done = bf16[1024,2560]{1,0:T(8,128)(2,1)} async-done(((bf16[128,2560]{1,0:T(8,128)(2,1)}), bf16[1024,2560]{1,0:T(8,128)(2,1)}) %all-gather.5.cloned.1.call-update) | async-done | bytes 5242896 | tf_op jit(solution)/shard_map/all_gather | solution.py:95
  1183.7 6.1 convolution_multiply_fusion.2
  1195.6 8.4 fusion.6
  1209.3 6.6 copy.22
  1215.9 6.5 reshape.23
  (321 shorter events, 294.6 us)
Async XLA Ops:
  7.2 255.8 %all-gather.3.cloned.1.call-start = ((), (), s32[]{:S(2)}) async-start(), calls=%async_computation.1 | async-start | bytes 14745600 | tf_op jit(solution)/shard_map/all_gather | solution.py:25
  7.9 1048.2 %all-reduce.3.cloned.1.call-start = ((), (), s32[]{:S(2)}) async-start(), calls=%async_computation.3 | async-start | bytes 2621440 | tf_op jit(solution)/shard_map/psum | solution.py:91
  273.0 12.8 %collective-permute-start.1 = (bf16[32,2560]{1,0:T(8,128)(2,1)S(1)}, bf16[32,2560]{1,0:T(8,128)(2,1)S(1)}, u32[]{:S(2)}, u32[]{:S(2)}) collective-permute-start(bf16[32,2560]{1,0:T(8,128)(2,1)S(1)} %get-tuple-element.375), channel_id=1, source_target_pairs={{8,0},{16,8},{24,16},{32,24},{40,32},{48,40},{56,48},{64,56},{72,6... | collective-permute-start | bytes 491528 | tf_op jit(solution)/shard_map/while/body/eval_jaxpr/ppermute | solution.py:12
  356.9 16.6 %collective-permute-start.1 = (bf16[32,2560]{1,0:T(8,128)(2,1)S(1)}, bf16[32,2560]{1,0:T(8,128)(2,1)S(1)}, u32[]{:S(2)}, u32[]{:S(2)}) collective-permute-start(bf16[32,2560]{1,0:T(8,128)(2,1)S(1)} %get-tuple-element.375), channel_id=1, source_target_pairs={{8,0},{16,8},{24,16},{32,24},{40,32},{48,40},{56,48},{64,56},{72,6... | collective-permute-start | bytes 491528 | tf_op jit(solution)/shard_map/while/body/eval_jaxpr/ppermute | solution.py:12
  358.8 13.7 %collective-permute-start = (bf16[32,2560]{1,0:T(8,128)(2,1)S(1)}, bf16[32,2560]{1,0:T(8,128)(2,1)S(1)}, u32[]{:S(2)}, u32[]{:S(2)}) collective-permute-start(bf16[32,2560]{1,0:T(8,128)(2,1)S(1)} %get-tuple-element.373), channel_id=1, source_target_pairs={{0,8},{8,16},{16,24},{24,32},{32,40},{40,48},{48,56},{56,64},{64,7... | collective-permute-start | bytes 491528 | tf_op jit(solution)/shard_map/while/body/eval_jaxpr/ppermute | solution.py:12
  385.2 11.0 collective-permute-start.1
  407.8 16.6 %collective-permute-start.1 = (bf16[32,2560]{1,0:T(8,128)(2,1)S(1)}, bf16[32,2560]{1,0:T(8,128)(2,1)S(1)}, u32[]{:S(2)}, u32[]{:S(2)}) collective-permute-start(bf16[32,2560]{1,0:T(8,128)(2,1)S(1)} %get-tuple-element.375), channel_id=1, source_target_pairs={{8,0},{16,8},{24,16},{32,24},{40,32},{48,40},{56,48},{64,56},{72,6... | collective-permute-start | bytes 491528 | tf_op jit(solution)/shard_map/while/body/eval_jaxpr/ppermute | solution.py:12
  409.7 13.7 %collective-permute-start = (bf16[32,2560]{1,0:T(8,128)(2,1)S(1)}, bf16[32,2560]{1,0:T(8,128)(2,1)S(1)}, u32[]{:S(2)}, u32[]{:S(2)}) collective-permute-start(bf16[32,2560]{1,0:T(8,128)(2,1)S(1)} %get-tuple-element.373), channel_id=1, source_target_pairs={{0,8},{8,16},{16,24},{24,32},{32,40},{40,48},{48,56},{56,64},{64,7... | collective-permute-start | bytes 491528 | tf_op jit(solution)/shard_map/while/body/eval_jaxpr/ppermute | solution.py:12
  436.1 11.0 collective-permute-start.1
  458.7 16.6 %collective-permute-start.1 = (bf16[32,2560]{1,0:T(8,128)(2,1)S(1)}, bf16[32,2560]{1,0:T(8,128)(2,1)S(1)}, u32[]{:S(2)}, u32[]{:S(2)}) collective-permute-start(bf16[32,2560]{1,0:T(8,128)(2,1)S(1)} %get-tuple-element.375), channel_id=1, source_target_pairs={{8,0},{16,8},{24,16},{32,24},{40,32},{48,40},{56,48},{64,56},{72,6... | collective-permute-start | bytes 491528 | tf_op jit(solution)/shard_map/while/body/eval_jaxpr/ppermute | solution.py:12
  460.6 13.7 %collective-permute-start = (bf16[32,2560]{1,0:T(8,128)(2,1)S(1)}, bf16[32,2560]{1,0:T(8,128)(2,1)S(1)}, u32[]{:S(2)}, u32[]{:S(2)}) collective-permute-start(bf16[32,2560]{1,0:T(8,128)(2,1)S(1)} %get-tuple-element.373), channel_id=1, source_target_pairs={{0,8},{8,16},{16,24},{24,32},{32,40},{40,48},{48,56},{56,64},{64,7... | collective-permute-start | bytes 491528 | tf_op jit(solution)/shard_map/while/body/eval_jaxpr/ppermute | solution.py:12
  487.0 18.8 %collective-permute-start.1 = (bf16[32,2560]{1,0:T(8,128)(2,1)S(1)}, bf16[32,2560]{1,0:T(8,128)(2,1)S(1)}, u32[]{:S(2)}, u32[]{:S(2)}) collective-permute-start(bf16[32,2560]{1,0:T(8,128)(2,1)S(1)} %get-tuple-element.375), channel_id=1, source_target_pairs={{8,0},{16,8},{24,16},{32,24},{40,32},{48,40},{56,48},{64,56},{72,6... | collective-permute-start | bytes 491528 | tf_op jit(solution)/shard_map/while/body/eval_jaxpr/ppermute | solution.py:12
  488.9 15.9 %collective-permute-start = (bf16[32,2560]{1,0:T(8,128)(2,1)S(1)}, bf16[32,2560]{1,0:T(8,128)(2,1)S(1)}, u32[]{:S(2)}, u32[]{:S(2)}) collective-permute-start(bf16[32,2560]{1,0:T(8,128)(2,1)S(1)} %get-tuple-element.373), channel_id=1, source_target_pairs={{0,8},{8,16},{16,24},{24,32},{32,40},{40,48},{48,56},{56,64},{64,7... | collective-permute-start | bytes 491528 | tf_op jit(solution)/shard_map/while/body/eval_jaxpr/ppermute | solution.py:12
  506.9 13.6 %collective-permute-start.1 = (bf16[32,2560]{1,0:T(8,128)(2,1)S(1)}, bf16[32,2560]{1,0:T(8,128)(2,1)S(1)}, u32[]{:S(2)}, u32[]{:S(2)}) collective-permute-start(bf16[32,2560]{1,0:T(8,128)(2,1)S(1)} %get-tuple-element.375), channel_id=1, source_target_pairs={{8,0},{16,8},{24,16},{32,24},{40,32},{48,40},{56,48},{64,56},{72,6... | collective-permute-start | bytes 491528 | tf_op jit(solution)/shard_map/while/body/eval_jaxpr/ppermute | solution.py:12
  508.8 10.7 collective-permute-start
  521.5 19.3 %collective-permute-start.1 = (bf16[32,2560]{1,0:T(8,128)(2,1)S(1)}, bf16[32,2560]{1,0:T(8,128)(2,1)S(1)}, u32[]{:S(2)}, u32[]{:S(2)}) collective-permute-start(bf16[32,2560]{1,0:T(8,128)(2,1)S(1)} %get-tuple-element.375), channel_id=1, source_target_pairs={{8,0},{16,8},{24,16},{32,24},{40,32},{48,40},{56,48},{64,56},{72,6... | collective-permute-start | bytes 491528 | tf_op jit(solution)/shard_map/while/body/eval_jaxpr/ppermute | solution.py:12
  523.5 16.4 %collective-permute-start = (bf16[32,2560]{1,0:T(8,128)(2,1)S(1)}, bf16[32,2560]{1,0:T(8,128)(2,1)S(1)}, u32[]{:S(2)}, u32[]{:S(2)}) collective-permute-start(bf16[32,2560]{1,0:T(8,128)(2,1)S(1)} %get-tuple-element.373), channel_id=1, source_target_pairs={{0,8},{8,16},{16,24},{24,32},{32,40},{40,48},{48,56},{56,64},{64,7... | collective-permute-start | bytes 491528 | tf_op jit(solution)/shard_map/while/body/eval_jaxpr/ppermute | solution.py:12
  541.9 13.6 %collective-permute-start.1 = (bf16[32,2560]{1,0:T(8,128)(2,1)S(1)}, bf16[32,2560]{1,0:T(8,128)(2,1)S(1)}, u32[]{:S(2)}, u32[]{:S(2)}) collective-permute-start(bf16[32,2560]{1,0:T(8,128)(2,1)S(1)} %get-tuple-element.375), channel_id=1, source_target_pairs={{8,0},{16,8},{24,16},{32,24},{40,32},{48,40},{56,48},{64,56},{72,6... | collective-permute-start | bytes 491528 | tf_op jit(solution)/shard_map/while/body/eval_jaxpr/ppermute | solution.py:12
  543.9 10.7 collective-permute-start
  556.6 13.6 %collective-permute-start.1 = (bf16[32,2560]{1,0:T(8,128)(2,1)S(1)}, bf16[32,2560]{1,0:T(8,128)(2,1)S(1)}, u32[]{:S(2)}, u32[]{:S(2)}) collective-permute-start(bf16[32,2560]{1,0:T(8,128)(2,1)S(1)} %get-tuple-element.375), channel_id=1, source_target_pairs={{8,0},{16,8},{24,16},{32,24},{40,32},{48,40},{56,48},{64,56},{72,6... | collective-permute-start | bytes 491528 | tf_op jit(solution)/shard_map/while/body/eval_jaxpr/ppermute | solution.py:12
  558.5 10.7 collective-permute-start
  571.2 13.6 %collective-permute-start.1 = (bf16[32,2560]{1,0:T(8,128)(2,1)S(1)}, bf16[32,2560]{1,0:T(8,128)(2,1)S(1)}, u32[]{:S(2)}, u32[]{:S(2)}) collective-permute-start(bf16[32,2560]{1,0:T(8,128)(2,1)S(1)} %get-tuple-element.375), channel_id=1, source_target_pairs={{8,0},{16,8},{24,16},{32,24},{40,32},{48,40},{56,48},{64,56},{72,6... | collective-permute-start | bytes 491528 | tf_op jit(solution)/shard_map/while/body/eval_jaxpr/ppermute | solution.py:12
  573.1 10.7 collective-permute-start
  585.9 13.6 %collective-permute-start.1 = (bf16[32,2560]{1,0:T(8,128)(2,1)S(1)}, bf16[32,2560]{1,0:T(8,128)(2,1)S(1)}, u32[]{:S(2)}, u32[]{:S(2)}) collective-permute-start(bf16[32,2560]{1,0:T(8,128)(2,1)S(1)} %get-tuple-element.375), channel_id=1, source_target_pairs={{8,0},{16,8},{24,16},{32,24},{40,32},{48,40},{56,48},{64,56},{72,6... | collective-permute-start | bytes 491528 | tf_op jit(solution)/shard_map/while/body/eval_jaxpr/ppermute | solution.py:12
  587.8 10.7 collective-permute-start
  600.5 13.6 %collective-permute-start.1 = (bf16[32,2560]{1,0:T(8,128)(2,1)S(1)}, bf16[32,2560]{1,0:T(8,128)(2,1)S(1)}, u32[]{:S(2)}, u32[]{:S(2)}) collective-permute-start(bf16[32,2560]{1,0:T(8,128)(2,1)S(1)} %get-tuple-element.375), channel_id=1, source_target_pairs={{8,0},{16,8},{24,16},{32,24},{40,32},{48,40},{56,48},{64,56},{72,6... | collective-permute-start | bytes 491528 | tf_op jit(solution)/shard_map/while/body/eval_jaxpr/ppermute | solution.py:12
  602.5 10.7 collective-permute-start
  615.2 13.6 %collective-permute-start.1 = (bf16[32,2560]{1,0:T(8,128)(2,1)S(1)}, bf16[32,2560]{1,0:T(8,128)(2,1)S(1)}, u32[]{:S(2)}, u32[]{:S(2)}) collective-permute-start(bf16[32,2560]{1,0:T(8,128)(2,1)S(1)} %get-tuple-element.375), channel_id=1, source_target_pairs={{8,0},{16,8},{24,16},{32,24},{40,32},{48,40},{56,48},{64,56},{72,6... | collective-permute-start | bytes 491528 | tf_op jit(solution)/shard_map/while/body/eval_jaxpr/ppermute | solution.py:12
  617.1 10.7 collective-permute-start
  629.8 13.6 %collective-permute-start.1 = (bf16[32,2560]{1,0:T(8,128)(2,1)S(1)}, bf16[32,2560]{1,0:T(8,128)(2,1)S(1)}, u32[]{:S(2)}, u32[]{:S(2)}) collective-permute-start(bf16[32,2560]{1,0:T(8,128)(2,1)S(1)} %get-tuple-element.375), channel_id=1, source_target_pairs={{8,0},{16,8},{24,16},{32,24},{40,32},{48,40},{56,48},{64,56},{72,6... | collective-permute-start | bytes 491528 | tf_op jit(solution)/shard_map/while/body/eval_jaxpr/ppermute | solution.py:12
  631.8 10.7 collective-permute-start
  644.5 13.6 %collective-permute-start.1 = (bf16[32,2560]{1,0:T(8,128)(2,1)S(1)}, bf16[32,2560]{1,0:T(8,128)(2,1)S(1)}, u32[]{:S(2)}, u32[]{:S(2)}) collective-permute-start(bf16[32,2560]{1,0:T(8,128)(2,1)S(1)} %get-tuple-element.375), channel_id=1, source_target_pairs={{8,0},{16,8},{24,16},{32,24},{40,32},{48,40},{56,48},{64,56},{72,6... | collective-permute-start | bytes 491528 | tf_op jit(solution)/shard_map/while/body/eval_jaxpr/ppermute | solution.py:12
  646.4 10.7 collective-permute-start
  659.1 13.6 %collective-permute-start.1 = (bf16[32,2560]{1,0:T(8,128)(2,1)S(1)}, bf16[32,2560]{1,0:T(8,128)(2,1)S(1)}, u32[]{:S(2)}, u32[]{:S(2)}) collective-permute-start(bf16[32,2560]{1,0:T(8,128)(2,1)S(1)} %get-tuple-element.375), channel_id=1, source_target_pairs={{8,0},{16,8},{24,16},{32,24},{40,32},{48,40},{56,48},{64,56},{72,6... | collective-permute-start | bytes 491528 | tf_op jit(solution)/shard_map/while/body/eval_jaxpr/ppermute | solution.py:12
  661.1 10.7 collective-permute-start
  673.8 13.6 %collective-permute-start.1 = (bf16[32,2560]{1,0:T(8,128)(2,1)S(1)}, bf16[32,2560]{1,0:T(8,128)(2,1)S(1)}, u32[]{:S(2)}, u32[]{:S(2)}) collective-permute-start(bf16[32,2560]{1,0:T(8,128)(2,1)S(1)} %get-tuple-element.375), channel_id=1, source_target_pairs={{8,0},{16,8},{24,16},{32,24},{40,32},{48,40},{56,48},{64,56},{72,6... | collective-permute-start | bytes 491528 | tf_op jit(solution)/shard_map/while/body/eval_jaxpr/ppermute | solution.py:12
  675.7 10.7 collective-permute-start
  688.5 13.6 %collective-permute-start.1 = (bf16[32,2560]{1,0:T(8,128)(2,1)S(1)}, bf16[32,2560]{1,0:T(8,128)(2,1)S(1)}, u32[]{:S(2)}, u32[]{:S(2)}) collective-permute-start(bf16[32,2560]{1,0:T(8,128)(2,1)S(1)} %get-tuple-element.375), channel_id=1, source_target_pairs={{8,0},{16,8},{24,16},{32,24},{40,32},{48,40},{56,48},{64,56},{72,6... | collective-permute-start | bytes 491528 | tf_op jit(solution)/shard_map/while/body/eval_jaxpr/ppermute | solution.py:12
  690.4 10.7 collective-permute-start
  703.1 110.3 %collective-permute-start.1 = (bf16[32,2560]{1,0:T(8,128)(2,1)S(1)}, bf16[32,2560]{1,0:T(8,128)(2,1)S(1)}, u32[]{:S(2)}, u32[]{:S(2)}) collective-permute-start(bf16[32,2560]{1,0:T(8,128)(2,1)S(1)} %get-tuple-element.375), channel_id=1, source_target_pairs={{8,0},{16,8},{24,16},{32,24},{40,32},{48,40},{56,48},{64,56},{72,6... | collective-permute-start | bytes 491528 | tf_op jit(solution)/shard_map/while/body/eval_jaxpr/ppermute | solution.py:12
  705.1 107.4 %collective-permute-start = (bf16[32,2560]{1,0:T(8,128)(2,1)S(1)}, bf16[32,2560]{1,0:T(8,128)(2,1)S(1)}, u32[]{:S(2)}, u32[]{:S(2)}) collective-permute-start(bf16[32,2560]{1,0:T(8,128)(2,1)S(1)} %get-tuple-element.373), channel_id=1, source_target_pairs={{0,8},{8,16},{16,24},{24,32},{32,40},{40,48},{48,56},{56,64},{64,7... | collective-permute-start | bytes 491528 | tf_op jit(solution)/shard_map/while/body/eval_jaxpr/ppermute | solution.py:12
  823.2 14.1 %collective-permute-start.1 = (bf16[32,2560]{1,0:T(8,128)(2,1)S(1)}, bf16[32,2560]{1,0:T(8,128)(2,1)S(1)}, u32[]{:S(2)}, u32[]{:S(2)}) collective-permute-start(bf16[32,2560]{1,0:T(8,128)(2,1)S(1)} %get-tuple-element.375), channel_id=1, source_target_pairs={{8,0},{16,8},{24,16},{32,24},{40,32},{48,40},{56,48},{64,56},{72,6... | collective-permute-start | bytes 491528 | tf_op jit(solution)/shard_map/while/body/eval_jaxpr/ppermute | solution.py:12
  825.1 11.1 collective-permute-start
  846.9 17.6 %collective-permute-start.1 = (bf16[32,2560]{1,0:T(8,128)(2,1)S(1)}, bf16[32,2560]{1,0:T(8,128)(2,1)S(1)}, u32[]{:S(2)}, u32[]{:S(2)}) collective-permute-start(bf16[32,2560]{1,0:T(8,128)(2,1)S(1)} %get-tuple-element.375), channel_id=1, source_target_pairs={{8,0},{16,8},{24,16},{32,24},{40,32},{48,40},{56,48},{64,56},{72,6... | collective-permute-start | bytes 491528 | tf_op jit(solution)/shard_map/while/body/eval_jaxpr/ppermute | solution.py:12
  848.9 14.7 %collective-permute-start = (bf16[32,2560]{1,0:T(8,128)(2,1)S(1)}, bf16[32,2560]{1,0:T(8,128)(2,1)S(1)}, u32[]{:S(2)}, u32[]{:S(2)}) collective-permute-start(bf16[32,2560]{1,0:T(8,128)(2,1)S(1)} %get-tuple-element.373), channel_id=1, source_target_pairs={{0,8},{8,16},{16,24},{24,32},{32,40},{40,48},{48,56},{56,64},{64,7... | collective-permute-start | bytes 491528 | tf_op jit(solution)/shard_map/while/body/eval_jaxpr/ppermute | solution.py:12
  874.3 12.2 collective-permute-start.1
  916.0 267.7 %all-gather.5.cloned.1.call-start = ((), (), s32[]{:S(2)}) async-start(), calls=%async_computation.2 | async-start | bytes 5898240 | tf_op jit(solution)/shard_map/all_gather | solution.py:95
  918.6 140.7 %all-to-all-start = ((bf16[128,8,320]{0,2,1:T(8,128)(2,1)}), bf16[128,8,320]{0,2,1:T(8,128)(2,1)S(1)}, u32[]{:S(2)}, u32[]{:S(2)}) async-start(bf16[128,8,320]{0,2,1:T(8,128)(2,1)} %copy.18), calls=%async_computation | async-start | bytes 1310720 | tf_op jit(solution)/shard_map/all_to_all | solution.py:94
  (30 other events, 1421.1 us)
Sparse Core Ops, SparseCore 0:
  10.6 252.2 all-gather.2
  916.1 140.0 all-reduce.2
  1059.3 124.3 all-gather.4
where the time goes:
time: 1240 us; the launch traced here: 1230 us
  waiting for transfers between devices  591 us (48%)
  starting transfers between devices  433 us (35%)
  matrix products  88.8 us (7%)
  other arithmetic  75.6 us (6%)
  local copies, waits for them, and re-layouts  25.7 us (2%)
  between operations  13.8 us (1%)
    ppermute x70, starting transfers between devices, from_behind(): return lax.ppermute(value, axis, pairs)  430 us
    all_gather x1, waiting for transfers between devices, local(): gathered = lax.all_gather(weight, 'dp', axis=1, tiled=True)[0]  255 us
    psum x1, waiting for transfers between devices, local(): lax.psum(a_local.astype(jnp.bfloat16), 'dp').astype(jnp.float32)  134 us
    all_gather x1, waiting for transfers between devices, local(): every_row = lax.all_gather(flat_cotangents, 'dp', axis=0, tiled=True)  124 us
    ppermute x70, waiting for transfers between devices, from_behind(): return lax.ppermute(value, axis, pairs)  76 us
    dynamic_update_slice x35, other arithmetic, backward_work(): lax.dynamic_update_index_in_dim(kept_rows, jnp.where(in_use, entering, pr...  34.6 us
    dot_general x4, matrix products, backward_layer(): lax.dot_general(values, gathered, (((1,), (1,)), ((), ())), preferred_ele...  34.5 us
    dynamic_update_slice x35, other arithmetic, forward_work(): lax.dynamic_update_index_in_dim(kept_rows, jnp.where(in_use, entering, pr...  34.4 us
  transfers between devices with their start and end apart: 74, of which 38 were waited for; matrix products, arithmetic and copies ran while one was open for 3% of the time, Pallas kernels for 0%

commit v1 on v0

v1 whole, which is shorter than its diff:
```python
import functools
import math

import jax
import jax.numpy as jnp
from jax import lax
from jax.experimental import pallas as pl
from jax.experimental.pallas import tpu as pltpu
from jax.sharding import PartitionSpec as P

MESH = pl.DeviceIdType.MESH
F32 = jnp.float32
BF16 = jnp.bfloat16
WD = 2560
HALF = WD // 2
ROWS = WD // 8
BLK = 64
NB = 40
WIN = 384
MICRO = 8
M = 32
GROUP = MICRO * M
TOK = 4 * GROUP
SCALE = 0.25 / math.sqrt(WD)
SECTIONS = 32


def lanes(start, size):
    return pl.ds(pl.multiple_of(start, 128), size)


def rows(start, size):
    return pl.ds(pl.multiple_of(start, 64), size)


def kernel(
    x_in, c_in, w_in, a_inv, g_inv,
    w_out, a_out, g_out,
    full_w, half_w, near, far, whole, half_in, half_out, part_out, acc,
    x_win, c_all, x_t,
    gat_send, gat_recv, start_send, start_recv,
    near_send, near_recv, far_send, far_recv, half_send, half_recv,
    ex_send, ex_recv, fac_send, fac_recv,
):
    section = lax.axis_index("section")
    dp = lax.axis_index("dp")
    core = lax.rem(section, 2)
    pair = section // 2
    hi = dp // 4
    y = lax.rem(dp, 4)
    other_hi = 1 - hi
    beside = 4 * other_hi + y
    mate = section + 1 - 2 * core
    outer = section - 1 + 2 * core
    at_end = jnp.logical_or(outer < 0, outer >= SECTIONS)
    even = core == 0
    mine = lanes(hi * HALF, HALF)
    others = lanes(other_hi * HALF, HALF)

    def across(step):
        return lax.rem(y + step, 4)

    def copy(src, dst, send, recv, target):
        return pltpu.make_async_remote_copy(
            src_ref=src, dst_ref=dst, send_sem=send, recv_sem=recv,
            device_id=target, device_id_type=MESH,
        )

    barrier = pltpu.get_barrier_semaphore()

    def greet(target):
        pl.semaphore_signal(barrier, inc=1, device_id=target, device_id_type=MESH)

    for step in (1, 2, 3):
        greet((section, 4 * hi + across(step)))
        greet((section, 4 * other_hi + across(step)))
    greet((section, beside))
    greet((mate, dp))

    @pl.when(jnp.logical_not(at_end))
    def _():
        greet((outer, dp))
        greet((outer, beside))
        pl.semaphore_wait(barrier, 10)

    @pl.when(at_end)
    def _():
        pl.semaphore_wait(barrier, 8)

    def piece(owner):
        return full_w.at[rows(owner * ROWS, ROWS), :]

    def strip(owner_y):
        return half_w.at[rows(owner_y * ROWS, ROWS), :]

    @pl.when(even)
    def _():
        side = copy(w_in.at[:, others], piece(dp), gat_send.at[6], gat_recv.at[6], (section, beside))
        side.start()
        sends = []
        for step in (1, 2, 3):
            sends.append(copy(
                w_in.at[:, mine], piece(dp), gat_send.at[step - 1], gat_recv.at[step - 1],
                (section, 4 * hi + across(step)),
            ))
            sends[-1].start()
        full_w[rows(dp * ROWS, ROWS), :] = w_in[:, mine]
        side.wait_recv()
        for step in (1, 2, 3):
            sends.append(copy(
                piece(beside), piece(beside), gat_send.at[step + 2], gat_recv.at[step + 2],
                (section, 4 * hi + across(step)),
            ))
            sends[-1].start()
        for one in sends:
            one.wait_recv()

        @pl.loop(0, 10)
        def _(i):
            half_w[:, lanes(i * 256, 256)] = full_w[rows(i * 256, 256), :].T

        side.wait_send()
        for one in sends:
            one.wait_send()

    @pl.when(jnp.logical_not(even))
    def _():
        sends = []
        for step in (1, 2, 3):
            sends.append(copy(
                w_in, strip(y), gat_send.at[step - 1], gat_recv.at[step - 1],
                (section, 4 * hi + across(step)),
            ))
            sends[-1].start()
        half_w[rows(y * ROWS, ROWS), :] = w_in[...]
        for one in sends:
            one.wait_recv()

        @pl.loop(0, 10)
        def _(i):
            full_w[rows(i * 256, 256), :] = half_w[:, lanes(i * 256, 256)].T

        for one in sends:
            one.wait_send()

    def begin(source):
        own = copy(source, whole.at[pl.ds(4 * hi, 4)], start_send, start_recv, (section, beside))
        own.start()
        whole[pl.ds(4 * hi, 4)] = source[...]
        own.wait()

    @pl.when(jnp.logical_and(at_end, even))
    def _():
        begin(x_in)

    @pl.when(jnp.logical_and(at_end, jnp.logical_not(even)))
    def _():
        begin(c_in)

    def to_mate(k):
        return copy(half_out.at[k], half_in.at[k], half_send.at[k], half_recv.at[k], (mate, dp))

    def to_near(k):
        return copy(part_out.at[k], near.at[k], near_send.at[k], near_recv.at[k], (outer, dp))

    def to_far(k):
        return copy(part_out.at[k], far.at[k], far_send.at[k], far_recv.at[k], (outer, beside))

    def from_whole():
        @pl.loop(0, MICRO)
        def _(k):
            @pl.when(jnp.logical_not(at_end))
            def _():
                to_near(k).wait_recv()
                to_far(k).wait_recv()
                whole[k] = (near[k].astype(F32) + far[k].astype(F32)).astype(BF16)

            for n in range(5):
                acc[:, n * 256:(n + 1) * 256] = jnp.dot(
                    whole[k], full_w[:, n * 256:(n + 1) * 256], preferred_element_type=F32
                )
            half_out[k] = (whole[k, :, mine].astype(F32) + SCALE * acc[:, :HALF]).astype(BF16)
            to_mate(k).start()

    def from_half():
        @pl.loop(0, MICRO)
        def _(k):
            to_mate(k).wait_recv()
            for n in range(5):
                acc[:, n * 512:(n + 1) * 512] = jnp.dot(
                    half_in[k], half_w[:, n * 512:(n + 1) * 512], preferred_element_type=F32
                )
            part_out[k] = (SCALE * acc[...]).astype(BF16)
            part_out[k, :, mine] = (half_in[k].astype(F32) + SCALE * acc[:, mine]).astype(BF16)

            @pl.when(jnp.logical_not(at_end))
            def _():
                to_near(k).start()
                to_far(k).start()

    whole_first = (pair < SECTIONS // 4) == even

    @pl.when(whole_first)
    def _():
        from_whole()

    from_half()

    @pl.when(jnp.logical_not(whole_first))
    def _():
        from_whole()

    def window(owner):
        return 320 * owner - 64 * lax.rem(owner, 2)

    spread = []

    def exchange_window(source, slot):
        sends = []
        for step in (1, 2, 3):
            to = across(step)
            sends.append(copy(
                source(to), x_win.at[y], ex_send.at[step - 1], ex_recv.at[step - 1],
                (section, 4 * hi + to),
            ))
            sends[-1].start()
        return sends

    @pl.when(even)
    def _():
        def view(to):
            return whole.at[:, :, lanes(window(4 * hi + to), WIN)]

        sends = exchange_window(view, None)
        x_win[y] = whole[:, :, lanes(window(dp), WIN)]
        side = copy(
            half_in, c_all.at[y, :, :, mine], ex_send.at[9], ex_recv.at[9], (section, beside)
        )
        side.start()
        for step in (1, 2, 3):
            sends.append(copy(
                half_in, c_all.at[y, :, :, mine], ex_send.at[step + 2], ex_recv.at[step + 2],
                (section, 4 * hi + across(step)),
            ))
            sends[-1].start()
        c_all[y, :, :, mine] = half_in[...]
        side.wait_recv()
        for step in (1, 2, 3):
            sends.append(copy(
                c_all.at[y, :, :, others], c_all.at[y, :, :, others],
                ex_send.at[step + 5], ex_recv.at[step + 5], (section, 4 * hi + across(step)),
            ))
            sends[-1].start()
        for one in sends:
            one.wait_recv()
        side.wait_send()
        for one in sends:
            one.wait_send()

    @pl.when(jnp.logical_not(even))
    def _():
        def view(to):
            return half_in.at[:, :, lanes(window(to), WIN)]

        sends = exchange_window(view, None)
        x_win[y] = half_in[:, :, lanes(window(y), WIN)]
        for step in (1, 2, 3):
            sends.append(copy(
                whole, c_all.at[y], ex_send.at[step + 2], ex_recv.at[step + 2],
                (section, 4 * hi + across(step)),
            ))
            sends[-1].start()
        c_all[y] = whole[...]
        for one in sends:
            one.wait()

    for g in range(4):
        x_t[:, g * GROUP:(g + 1) * GROUP] = x_win[g].reshape(GROUP, WIN).T
    own_rows = rows(64 * lax.rem(y, 2), ROWS)

    def select(height, width):
        return (
            lax.rem(lax.broadcasted_iota(jnp.int32, (height, width), 0), 64)
            == lax.rem(lax.broadcasted_iota(jnp.int32, (height, width), 1), 64)
        )

    def same_block(size):
        return (
            lax.broadcasted_iota(jnp.int32, (size, size), 0) // 64
            == lax.broadcasted_iota(jnp.int32, (size, size), 1) // 64
        )

    def fold(gram):
        size = gram.shape[0]
        kept = jnp.where(same_block(size), gram, 0.0)
        return jnp.dot(
            kept, select(size, 64).astype(F32), precision=lax.Precision.HIGHEST,
            preferred_element_type=F32,
        )

    def unfold(blocks):
        size = blocks.shape[0]
        tiled = jnp.dot(blocks, select(64, size).astype(BF16), preferred_element_type=F32)
        return jnp.where(same_block(size), tiled, 0.0).astype(BF16)

    def contract(a, b):
        return lax.dot_general(a, b, (((1,), (1,)), ((), ())), preferred_element_type=F32)

    own = x_t[own_rows, :]
    own_blocks = rows(dp * ROWS, ROWS)
    a_out[own_blocks, :] = fold(contract(own, own) / TOK)
    shares = []
    for index in range(7):
        step = index % 4 if index < 4 else index - 3
        target_hi = other_hi if index < 4 else hi
        one = copy(
            a_out.at[own_blocks, :], a_out.at[own_blocks, :], fac_send.at[index], fac_recv.at[index],
            (section, 4 * target_hi + across(step)),
        )
        one.start()
        shares.append(one)

    left = unfold(a_inv[...])

    @pl.loop(0, 10)
    def _(n):
        cols = lanes(n * 256, 256)
        c_cols = c_all[:, :, :, cols].reshape(TOK, 256)
        g_out[rows(n * 256, 256), :] = fold(jnp.dot(c_cols.T, c_cols, preferred_element_type=F32) / TOK)
        grad = jnp.dot(x_t[own_rows, :], c_cols, preferred_element_type=F32) / TOK
        halfway = jnp.dot(left, grad.astype(BF16), preferred_element_type=F32).astype(BF16)
        right = unfold(g_inv[rows(n * 256, 256), :])
        step = jnp.dot(halfway, right, preferred_element_type=F32)
        w_out[:, cols] = (w_in[:, cols].astype(F32) - step).astype(BF16)

    for one in shares:
        one.wait()

    @pl.loop(0, MICRO)
    def _(k):
        to_mate(k).wait_send()

        @pl.when(jnp.logical_not(at_end))
        def _():
            to_near(k).wait_send()
            to_far(k).wait_send()


def local(inputs, cotangent, weight, a_inv, g_inv):
    vmem = pl.BlockSpec(memory_space=pltpu.VMEM)
    dma = pltpu.SemaphoreType.DMA
    new_weight, a_fac, g_fac = pl.pallas_call(
        kernel,
        out_shape=(
            jax.ShapeDtypeStruct((ROWS, WD), BF16),
            jax.ShapeDtypeStruct((WD, BLK), F32),
            jax.ShapeDtypeStruct((WD, BLK), F32),
        ),
        in_specs=[vmem] * 5,
        out_specs=(vmem,) * 3,
        scratch_shapes=[
            pltpu.VMEM((WD, HALF), BF16),
            pltpu.VMEM((HALF, WD), BF16),
            pltpu.VMEM((MICRO, M, WD), BF16),
            pltpu.VMEM((MICRO, M, WD), BF16),
            pltpu.VMEM((MICRO, M, WD), BF16),
            pltpu.VMEM((MICRO, M, HALF), BF16),
            pltpu.VMEM((MICRO, M, HALF), BF16),
            pltpu.VMEM((MICRO, M, WD), BF16),
            pltpu.VMEM((M, WD), F32),
            pltpu.VMEM((4, MICRO, M, WIN), BF16),
            pltpu.VMEM((4, MICRO, M, WD), BF16),
            pltpu.VMEM((WIN, TOK), BF16),
            dma((7,)), dma((7,)), dma, dma,
            dma((MICRO,)), dma((MICRO,)), dma((MICRO,)), dma((MICRO,)),
            dma((MICRO,)), dma((MICRO,)),
            dma((10,)), dma((10,)), dma((7,)), dma((7,)),
        ],
        compiler_params=pltpu.CompilerParams(
            collective_id=0, has_side_effects=True, vmem_limit_bytes=56 << 20
        ),
        cost_estimate=pl.CostEstimate(flops=6 << 30, bytes_accessed=8 << 20, transcendentals=0),
        name="kfac",
    )(
        inputs, cotangent, weight[0],
        a_inv[0].reshape(ROWS, BLK), g_inv[0].reshape(WD, BLK),
    )
    return (
        new_weight[None],
        a_fac.reshape(1, NB, BLK, BLK),
        g_fac.reshape(1, NB, BLK, BLK),
    )


def solution(mesh):
    placed = (
        P(None, "dp", None),
        P(None, "dp", None),
        P("section", "dp", None),
        P("section", "dp", None, None),
        P("section", None, None, None),
    )
    return jax.shard_map(
        local,
        mesh=mesh,
        in_specs=placed,
        out_specs=(
            P("section", "dp", None),
            P("section", None, None, None),
            P("section", None, None, None),
        ),
        check_vma=False,
    )
```

time: 1240 us -> 442 us (0.36)
  waiting for transfers between devices: 591 us -> 0 us
  starting transfers between devices: 433 us -> 0 us
  Pallas kernels: 0 us -> 430 us
  matrix products: 88.8 us -> 0 us
  other arithmetic: 75.6 us -> 0 us
  local copies, waits for them, and re-layouts: 25.7 us -> 5.65 us
  between operations: 13.8 us -> 0.65 us
    pallas_call x0 -> x1, Pallas kernels: none -> 430 us  [local(): pl.pallas_call(kernel, out_shape=(jax.ShapeDtypeStruct((ROWS, WD), BF16),...]
    ppermute x70 -> x0, starting transfers between devices: 430 us -> none  [from_behind(): return lax.ppermute(value, axis, pairs)]
    all_gather x2 -> x0, waiting for transfers between devices: 379 us -> none  [the longest x1 255 us: local(): gathered = lax.all_gather(weight, 'dp', axis=1, tiled=True)[0]]
    psum x1 -> x0, waiting for transfers between devices: 134 us -> none  [local(): lax.psum(a_local.astype(jnp.bfloat16), 'dp').astype(jnp.float32)]
    dot_general x13 -> x0, matrix products: 88.8 us -> none  [the longest x4 34.5 us: backward_layer(): lax.dot_general(values, gathered, (((1,), (1,)), ((), ())), preferred_ele...]
    ppermute x70 -> x0, waiting for transfers between devices: 76 us -> none  [from_behind(): return lax.ppermute(value, axis, pairs)]
    dynamic_update_slice x70 -> x0, other arithmetic: 69 us -> none  [the longest x35 34.6 us: backward_work(): lax.dynamic_update_index_in_dim(kept_rows, jnp.where(in_use, entering, pr...]
  transfers between devices with their start and end apart: 74 -> 0, of which waited for: 38 -> 0; matrix products, arithmetic and copies ran while one was open for 3% -> 0% of each run, Pallas kernels for 0% -> 0%
where the time goes in v1:
time: 442 us; the launch traced here: 436 us
  Pallas kernels  430 us (97%)
  local copies, waits for them, and re-layouts  5.65 us (1%)
    pallas_call x1, Pallas kernels, local(): pl.pallas_call(kernel, out_shape=(jax.ShapeDtypeStruct((ROWS, WD), BF16),...  430 us

profile of v1, /device:TPU:1, one launch (start us, length us, event | category | flops | bytes accessed | tf_op | source)
XLA Modules:
  0.0 436.3 jit_solution(18211859682810606851)
XLA Ops:
  0.6 430.0 %kfac.1 = (bf16[320,2560]{1,0:T(8,128)(2,1)}, f32[2560,64]{1,0:T(8,128)}, f32[2560,64]{1,0:T(8,128)}) custom-call(bf16[4,32,2560]{2,1,0:T(8,128)(2,1)} %x_in.1, bf16[4,32,2560]{2,1,0:T(8,128)(2,1)} %c_in.1, bf16[320,2560]{1,0:T(8,128)(2,1)} %bitcast.9, bf16[320,64]{1,0:T(8,128)(2,1)} %bitcast.11, bf16[2560,64]{1,0:T(8,128)(2,1)} %bitcast.10), custom_call_target="tpu_custom_call" | custom-call | flops 6442450944 | bytes 8388608 | tf_op jit(solution)/shard_map/kfac/pallas_call | solution.py:352
  430.7 0.0 copy-start.1
  430.7 2.8 copy.11
  433.5 0.0 copy-done.1
  433.5 0.0 copy-start
  433.5 1.1 copy.12
  434.5 0.7 copy-done
  435.3 1.1 copy.13
Async XLA Ops:
  430.7 2.8 copy-start.1
  433.5 1.8 copy-start

commit v2 on v1

v2 whole, which is shorter than its diff:
```python
import functools
import math

import jax
import jax.numpy as jnp
from jax import lax
from jax.experimental import pallas as pl
from jax.experimental.pallas import tpu as pltpu
from jax.sharding import PartitionSpec as P

MESH = pl.DeviceIdType.MESH
F32 = jnp.float32
BF16 = jnp.bfloat16
WD = 2560
ROWS = WD // 8
BLK = 64
NB = 40
WIN = 384
MICRO = 4
M = 32
GROUP = MICRO * M
TOK = 8 * GROUP
SCALE = 0.25 / math.sqrt(WD)
SECTIONS = 32
TURN = 8
LAG = 10
CUTS = tuple((start, 512) for start in range(0, WD, 512))


def lanes(start, size):
    return pl.ds(pl.multiple_of(start, 128), size)


def rows(start, size):
    return pl.ds(pl.multiple_of(start, 64), size)


def kernel(
    x_in, c_in, w_in, a_inv, g_inv,
    w_out, a_out, g_out,
    deep_w, wide_w, deep_in, wide_in, deep_out, wide_out, acc,
    x_win, c_all, x_t, fac,
    gat_send, gat_recv, deep_send, deep_recv, wide_send, wide_recv,
    x_send, x_recv, c_send, c_recv, fac_send, fac_recv,
):
    section = lax.axis_index("section")
    dp = lax.axis_index("dp")
    core = lax.rem(section, 2)
    pair = section // 2
    hi = dp // 4
    y = lax.rem(dp, 4)
    other_hi = 1 - hi
    beside = 4 * other_hi + y
    mate = section + 1 - 2 * core
    outer = section - 1 + 2 * core
    at_end = jnp.logical_or(outer < 0, outer >= SECTIONS)
    even = core == 0

    def across(step):
        return lax.rem(y + step, 4)

    def copy(src, dst, send, recv, target):
        return pltpu.make_async_remote_copy(
            src_ref=src, dst_ref=dst, send_sem=send, recv_sem=recv,
            device_id=target, device_id_type=MESH,
        )

    def peer(index):
        if index < 4:
            return (section, 4 * other_hi + across(index))
        return (section, 4 * hi + across(index - 3))

    barrier = pltpu.get_barrier_semaphore()

    def greet(target):
        pl.semaphore_signal(barrier, inc=1, device_id=target, device_id_type=MESH)

    for index in range(7):
        greet(peer(index))
    greet((mate, dp))

    @pl.when(jnp.logical_not(at_end))
    def _():
        greet((outer, dp))
        pl.semaphore_wait(barrier, 9)

    @pl.when(at_end)
    def _():
        pl.semaphore_wait(barrier, 8)

    ahead, behind = across(1), across(3)

    def ring(view, own, send, recv):
        def to(target_y, slot, ref, place):
            return copy(ref, place, send(slot), recv(slot), (section, 4 * hi + target_y))

        def link(slot):
            if slot < 2:
                return to((ahead, behind)[slot], slot, own, view(y))
            passed = view((behind, ahead)[slot - 2], slot - 2)
            return to((ahead, behind)[slot - 2], slot, passed, passed)

        return link

    def pass_on(links):
        links(0).wait_recv()
        links(2).start()
        links(1).wait_recv()
        links(3).start()

    def arrived(links):
        links(2).wait_recv()
        links(3).wait_recv()

    def sent(links):
        for slot in range(4):
            links(slot).wait_send()

    def gather_weight(full, flipped):
        def block(group, low, size):
            def view(owner, part=None):
                start = (4 * group + owner) * ROWS + low
                if part is None:
                    return full.at[pl.ds(pl.multiple_of(start, 32), size), :]
                half = size // 2
                return full.at[pl.ds(pl.multiple_of(start + part * half, 16), half), :]

            return view

        def links_of(view, own, base):
            return ring(
                view, own, lambda slot: gat_send.at[base + slot], lambda slot: gat_recv.at[base + slot]
            )

        half = ROWS // 2
        sides, rings = [], []
        for part in range(2):
            there = block(hi, part * half, half)(y)
            sides.append(copy(
                w_in.at[pl.ds(part * half, half), :], there,
                gat_send.at[12 + part], gat_recv.at[12 + part], (section, beside),
            ))
            sides[-1].start()
        close = links_of(block(hi, 0, ROWS), w_in, 0)
        close(0).start()
        close(1).start()
        full[rows(dp * ROWS, ROWS), :] = w_in[...]
        for part in range(2):
            view = block(other_hi, part * half, half)
            rings.append(links_of(view, view(y), 4 + 4 * part))

        def turn(group):
            for n in range(5):
                cols = lanes(group * 4 * ROWS + n * 256, 256)
                flipped[:, cols] = full[rows(group * 4 * ROWS + n * 256, 256), :].T

        sides[0].wait_recv()
        rings[0](0).start()
        rings[0](1).start()
        pass_on(close)
        sides[1].wait_recv()
        rings[1](0).start()
        rings[1](1).start()
        arrived(close)
        turn(hi)
        pass_on(rings[0])
        pass_on(rings[1])
        arrived(rings[0])
        arrived(rings[1])
        turn(other_hi)
        for one in sides:
            one.wait_send()
        for links in (close, rings[0], rings[1]):
            sent(links)

    @pl.when(even)
    def _():
        gather_weight(deep_w, wide_w)

    @pl.when(jnp.logical_not(even))
    def _():
        gather_weight(wide_w, deep_w)

    @pl.when(jnp.logical_and(at_end, even))
    def _():
        deep_in[...] = x_in[...]

    @pl.when(jnp.logical_and(at_end, jnp.logical_not(even)))
    def _():
        deep_in[...] = c_in[...]

    def to_mate(k):
        return copy(deep_out.at[k], wide_in.at[k], wide_send.at[k], wide_recv.at[k], (mate, dp))

    def to_outer(k, n):
        view = (k, slice(None), pl.ds(*CUTS[n]))
        return copy(
            wide_out.at[view], deep_in.at[view], deep_send.at[k, n], deep_recv.at[k, n], (outer, dp)
        )

    def window(owner):
        return 320 * owner - 64 * lax.rem(owner, 2)

    def x_link(k, index, source):
        return copy(
            source, x_win.at[dp, k], x_send.at[k, index], x_recv.at[k, index], peer(index)
        )

    def send_x(k, source):
        for index in range(7):
            start = window(peer(index)[1])
            x_link(k, index, source.at[k, :, lanes(start, WIN)]).start()
        x_win[dp, k] = source[k, :, lanes(window(dp), WIN)]

    def c_ring(k, group, base):
        def view(owner, part=None):
            if part is None:
                return c_all.at[4 * group + owner, k]
            return c_all.at[4 * group + owner, k, :, pl.ds(part * (WD // 2), WD // 2)]

        return ring(
            view, view(y), lambda slot: c_send.at[k, base + slot], lambda slot: c_recv.at[k, base + slot]
        )

    def c_side(k):
        view = c_all.at[dp, k]
        return copy(view, view, c_send.at[k, 8], c_recv.at[k, 8], (section, beside))

    def send_c(k, source):
        c_all[dp, k] = source[k]
        c_side(k).start()
        links = c_ring(k, hi, 0)
        links(0).start()
        links(1).start()

    def run_deep(k, is_even, is_end):
        for n, (start, size) in enumerate(CUTS):
            if not is_end:
                to_outer(k, n).wait_recv()
            term = jnp.dot(
                deep_in[k, :, start:start + size], deep_w[start:start + size, :],
                preferred_element_type=F32,
            )
            if n == 0:
                acc[...] = term
            else:
                acc[...] += term
        deep_out[k] = (deep_in[k].astype(F32) + SCALE * acc[...]).astype(BF16)
        to_mate(k).start()
        if is_even:
            send_x(k, deep_in)
        else:
            send_c(k, deep_in)

    def run_wide(k, is_even, is_end):
        to_mate(k).wait_recv()
        if not is_end:
            for n, (start, size) in enumerate(CUTS):
                term = jnp.dot(
                    wide_in[k], wide_w[:, start:start + size], preferred_element_type=F32
                )
                kept = wide_in[k, :, start:start + size].astype(F32)
                wide_out[k, :, start:start + size] = (kept + SCALE * term).astype(BF16)
                to_outer(k, n).start()
        if is_even:
            send_c(k, wide_in)
        else:
            send_x(k, wide_in)

    def by_place(work, k, allowed):
        for is_even in (True, False):
            for is_end in (True, False):
                here = jnp.logical_and(even == is_even, at_end == is_end)

                @pl.when(jnp.logical_and(allowed, here))
                def _():
                    work(k, is_even, is_end)

    def each(work):
        @pl.loop(0, MICRO)
        def _(k):
            work(k)

    def gather_c():
        def widen(k):
            c_side(k).wait_recv()
            links = c_ring(k, other_hi, 4)
            links(0).start()
            links(1).start()

        each(widen)
        each(lambda k: pass_on(c_ring(k, hi, 0)))
        each(lambda k: pass_on(c_ring(k, other_hi, 4)))

        def finish(k):
            arrived(c_ring(k, hi, 0))
            arrived(c_ring(k, other_hi, 4))

        each(finish)

    deep_first = (pair < TURN) == even
    early = pair >= 12
    gap = jnp.where(pair < TURN, 2 * TURN - 1 - 2 * pair, 2 * pair + 1 - 2 * TURN)
    lag = jnp.minimum(gap * LAG // 4, MICRO)
    deep_lag = jnp.where(deep_first, 0, lag)
    wide_lag = jnp.where(deep_first, lag, 0)

    @pl.loop(0, MICRO + lag)
    def _(t):
        def turn(work, late):
            k = t - late
            allowed = jnp.logical_and(k >= 0, k < MICRO)
            by_place(work, jnp.clip(k, 0, MICRO - 1), allowed)

        turn(run_deep, deep_lag)
        turn(run_wide, wide_lag)

        @pl.when(jnp.logical_and(early, t == MICRO - 1))
        def _():
            gather_c()

    def take_x(k):
        for index in range(7):
            x_link(k, index, x_win.at[dp, k]).wait_recv()

    each(take_x)

    @pl.when(jnp.logical_not(early))
    def _():
        gather_c()

    for g in range(8):
        x_t[:, g * GROUP:(g + 1) * GROUP] = x_win[g].reshape(GROUP, WIN).T
    own_rows = rows(64 * lax.rem(y, 2), ROWS)

    def select(height, width):
        return (
            lax.rem(lax.broadcasted_iota(jnp.int32, (height, width), 0), 64)
            == lax.broadcasted_iota(jnp.int32, (height, width), 1)
        )

    def same_block(size):
        return (
            lax.broadcasted_iota(jnp.int32, (size, size), 0) // 64
            == lax.broadcasted_iota(jnp.int32, (size, size), 1) // 64
        )

    def fold(gram, width=64):
        size = gram.shape[0]
        kept = jnp.where(same_block(size), gram, 0.0)
        return jnp.dot(
            kept, select(size, width).astype(F32), precision=lax.Precision.HIGHEST,
            preferred_element_type=F32,
        )

    def unfold(blocks):
        size = blocks.shape[0]
        tiled = lax.dot_general(
            blocks, select(size, 64).astype(BF16), (((1,), (1,)), ((), ())), preferred_element_type=F32
        )
        return jnp.where(same_block(size), tiled, 0.0).astype(BF16)

    def contract(a, b):
        return lax.dot_general(a, b, (((1,), (1,)), ((), ())), preferred_element_type=F32)

    own = x_t[own_rows, :]
    fac[dp] = fold(contract(own, own) / TOK, 128).astype(BF16)
    shares = []
    for index in range(7):
        one = copy(
            fac.at[dp], fac.at[dp], fac_send.at[index], fac_recv.at[index], peer(index)
        )
        one.start()
        shares.append(one)

    left = unfold(a_inv[...])

    @pl.loop(0, 10)
    def _(n):
        cols = lanes(n * 256, 256)
        c_cols = c_all[:, :, :, cols].reshape(TOK, 256)
        g_out[rows(n * 256, 256), :] = fold(jnp.dot(c_cols.T, c_cols, preferred_element_type=F32) / TOK)
        grad = jnp.dot(x_t[own_rows, :], c_cols, preferred_element_type=F32) / TOK
        halfway = jnp.dot(left, grad.astype(BF16), preferred_element_type=F32).astype(BF16)
        right = unfold(g_inv[rows(n * 256, 256), :])
        step = jnp.dot(halfway, right, preferred_element_type=F32)
        w_out[:, cols] = (w_in[:, cols].astype(F32) - step).astype(BF16)

    for one in shares:
        one.wait()
    for owner in range(8):
        a_out[owner * ROWS:(owner + 1) * ROWS, :] = fac[owner, :, :BLK].astype(F32)

    def close_sends(k):
        to_mate(k).wait_send()
        for index in range(7):
            x_link(k, index, x_win.at[dp, k]).wait_send()

        @pl.when(jnp.logical_not(at_end))
        def _():
            for n in range(len(CUTS)):
                to_outer(k, n).wait_send()

        c_side(k).wait_send()
        sent(c_ring(k, hi, 0))
        sent(c_ring(k, other_hi, 4))

    each(close_sends)


def local(inputs, cotangent, weight, a_inv, g_inv):
    vmem = pl.BlockSpec(memory_space=pltpu.VMEM)
    dma = pltpu.SemaphoreType.DMA
    held = pltpu.VMEM((MICRO, M, WD), BF16)
    new_weight, a_fac, g_fac = pl.pallas_call(
        kernel,
        out_shape=(
            jax.ShapeDtypeStruct((ROWS, WD), BF16),
            jax.ShapeDtypeStruct((WD, BLK), F32),
            jax.ShapeDtypeStruct((WD, BLK), F32),
        ),
        in_specs=[vmem] * 5,
        out_specs=(vmem,) * 3,
        scratch_shapes=[
            pltpu.VMEM((WD, WD), BF16),
            pltpu.VMEM((WD, WD), BF16),
            held, held, held, held,
            pltpu.VMEM((M, WD), F32),
            pltpu.VMEM((8, MICRO, M, WIN), BF16),
            pltpu.VMEM((8, MICRO, M, WD), BF16),
            pltpu.VMEM((WIN, TOK), BF16),
            pltpu.VMEM((8, ROWS, 128), BF16),
            dma((14,)), dma((14,)),
            dma((MICRO, len(CUTS))), dma((MICRO, len(CUTS))), dma((MICRO,)), dma((MICRO,)),
            dma((MICRO, 7)), dma((MICRO, 7)), dma((MICRO, 9)), dma((MICRO, 9)),
            dma((7,)), dma((7,)),
        ],
        compiler_params=pltpu.CompilerParams(
            collective_id=0, has_side_effects=True, vmem_limit_bytes=56 << 20
        ),
        cost_estimate=pl.CostEstimate(flops=6 << 30, bytes_accessed=8 << 20, transcendentals=0),
        name="kfac",
    )(
        inputs, cotangent, weight[0],
        a_inv[0].reshape(ROWS, BLK), g_inv[0].reshape(WD, BLK),
    )
    return (
        new_weight[None],
        a_fac.reshape(1, NB, BLK, BLK),
        g_fac.reshape(1, NB, BLK, BLK),
    )


def solution(mesh):
    placed = (
        P(None, "dp", None),
        P(None, "dp", None),
        P("section", "dp", None),
        P("section", "dp", None, None),
        P("section", None, None, None),
    )
    return jax.shard_map(
        local,
        mesh=mesh,
        in_specs=placed,
        out_specs=(
            P("section", "dp", None),
            P("section", None, None, None),
            P("section", None, None, None),
        ),
        check_vma=False,
    )
```

time: 442 us -> 348 us (0.79); the launches traced: 436 us -> 348 us
  Pallas kernels: 430 us -> 342 us
    pallas_call x1, Pallas kernels: 430 us -> 342 us  [local(): pl.pallas_call(kernel, out_shape=(jax.ShapeDtypeStruct((ROWS, WD), BF16),...]
where the time goes in v2:
time: 348 us
  Pallas kernels  342 us (98%)
  local copies, waits for them, and re-layouts  5.65 us (2%)
    pallas_call x1, Pallas kernels, local(): pl.pallas_call(kernel, out_shape=(jax.ShapeDtypeStruct((ROWS, WD), BF16),...  342 us

profile of v2, /device:TPU:1, one launch (start us, length us, event | category | flops | bytes accessed | tf_op | source)
XLA Modules:
  0.0 348.0 jit_solution(13401657209856582416)
XLA Ops:
  0.6 341.7 %kfac.1 = (bf16[320,2560]{1,0:T(8,128)(2,1)}, f32[2560,64]{1,0:T(8,128)}, f32[2560,64]{1,0:T(8,128)}) custom-call(bf16[4,32,2560]{2,1,0:T(8,128)(2,1)} %x_in.1, bf16[4,32,2560]{2,1,0:T(8,128)(2,1)} %c_in.1, bf16[320,2560]{1,0:T(8,128)(2,1)} %bitcast.9, bf16[320,64]{1,0:T(8,128)(2,1)} %bitcast.11, bf16[2560,64]{1,0:T(8,128)(2,1)} %bitcast.10), custom_call_target="tpu_custom_call" | custom-call | flops 6442450944 | bytes 8388608 | tf_op jit(solution)/shard_map/kfac/pallas_call | solution.py:415
  342.4 0.0 copy-start.1
  342.4 2.8 copy.11
  345.2 0.0 copy-done.1
  345.2 0.0 copy-start
  345.2 1.1 copy.12
  346.2 0.7 copy-done
  347.0 1.1 copy.13
Async XLA Ops:
  342.4 2.8 copy-start.1
  345.2 1.8 copy-start

commit v3 on v2

--- a/solution.py
+++ b/solution.py
@@ -24,6 +24,7 @@
 SECTIONS = 32
 TURN = 8
 LAG = 10
+TELL = 2
 CUTS = tuple((start, 512) for start in range(0, WD, 512))
 
 
@@ -41,12 +42,15 @@
     deep_w, wide_w, deep_in, wide_in, deep_out, wide_out, acc,
     x_win, c_all, x_t, fac,
     gat_send, gat_recv, deep_send, deep_recv, wide_send, wide_recv,
-    x_send, x_recv, c_send, c_recv, fac_send, fac_recv,
+    x_send, x_recv, c_send, c_recv, fac_send, fac_recv, passed,
 ):
     section = lax.axis_index("section")
     dp = lax.axis_index("dp")
     core = lax.rem(section, 2)
     pair = section // 2
+    plane = section // 8
+    early = plane == 3
+    middle = jnp.logical_and(plane > 0, plane < 3)
     hi = dp // 4
     y = lax.rem(dp, 4)
     other_hi = 1 - hi
@@ -78,15 +82,20 @@
     for index in range(7):
         greet(peer(index))
     greet((mate, dp))
+    teller = jnp.where(plane == 0, 8, jnp.where(plane == 1, 7, jnp.where(plane == 2, 24, 23)))
+    telling = jnp.logical_or(
+        jnp.logical_or(section == 7, section == 8), jnp.logical_or(section == 23, section == 24)
+    )
+
+    @pl.when(teller != outer)
+    def _():
+        greet((teller, dp))
 
     @pl.when(jnp.logical_not(at_end))
     def _():
         greet((outer, dp))
-        pl.semaphore_wait(barrier, 9)
-
-    @pl.when(at_end)
-    def _():
-        pl.semaphore_wait(barrier, 8)
+
+    pl.semaphore_wait(barrier, 8 + jnp.where(at_end, 0, 1) + jnp.where(telling, 7, 0))
 
     ahead, behind = across(1), across(3)
 
@@ -201,16 +210,23 @@
     def window(owner):
         return 320 * owner - 64 * lax.rem(owner, 2)
 
-    def x_link(k, index, source):
-        return copy(
-            source, x_win.at[dp, k], x_send.at[k, index], x_recv.at[k, index], peer(index)
-        )
-
-    def send_x(k, source):
+    def x_link(index, source):
+        return copy(source, x_win.at[dp], x_send.at[index], x_recv.at[index], peer(index))
+
+    def send_x(source):
         for index in range(7):
             start = window(peer(index)[1])
-            x_link(k, index, source.at[k, :, lanes(start, WIN)]).start()
-        x_win[dp, k] = source[k, :, lanes(window(dp), WIN)]
+            x_link(index, source.at[:, :, lanes(start, WIN)]).start()
+        x_win[dp] = source[:, :, lanes(window(dp), WIN)]
+
+    def send_own_x():
+        @pl.when(even)
+        def _():
+            send_x(deep_in)
+
+        @pl.when(jnp.logical_not(even))
+        def _():
+            send_x(wide_in)
 
     def c_ring(k, group, base):
         def view(owner, part=None):
@@ -228,10 +244,22 @@
 
     def send_c(k, source):
         c_all[dp, k] = source[k]
-        c_side(k).start()
         links = c_ring(k, hi, 0)
         links(0).start()
         links(1).start()
+
+        @pl.when(plane == 0)
+        def _():
+            c_side(k).start()
+
+    def widen(k):
+        c_side(k).wait_recv()
+        links = c_ring(k, other_hi, 4)
+        links(0).start()
+        links(1).start()
+
+    def pass_close(k):
+        pass_on(c_ring(k, hi, 0))
 
     def run_deep(k, is_even, is_end):
         for n, (start, size) in enumerate(CUTS):
@@ -247,9 +275,7 @@
                 acc[...] += term
         deep_out[k] = (deep_in[k].astype(F32) + SCALE * acc[...]).astype(BF16)
         to_mate(k).start()
-        if is_even:
-            send_x(k, deep_in)
-        else:
+        if not is_even:
             send_c(k, deep_in)
 
     def run_wide(k, is_even, is_end):
@@ -264,8 +290,6 @@
                 to_outer(k, n).start()
         if is_even:
             send_c(k, wide_in)
-        else:
-            send_x(k, wide_in)
 
     def by_place(work, k, allowed):
         for is_even in (True, False):
@@ -281,15 +305,18 @@
         def _(k):
             work(k)
 
-    def gather_c():
-        def widen(k):
-            c_side(k).wait_recv()
-            links = c_ring(k, other_hi, 4)
-            links(0).start()
-            links(1).start()
+    def gather_sides():
+        @pl.when(early)
+        def _():
+            each(lambda k: c_side(k).start())
 
         each(widen)
-        each(lambda k: pass_on(c_ring(k, hi, 0)))
+
+        @pl.when(jnp.logical_not(middle))
+        def _():
+            each(pass_close)
+
+    def gather_rest():
         each(lambda k: pass_on(c_ring(k, other_hi, 4)))
 
         def finish(k):
@@ -299,7 +326,13 @@
         each(finish)
 
     deep_first = (pair < TURN) == even
-    early = pair >= 12
+
+    def tell(teller, start):
+        @pl.when(section == teller)
+        def _():
+            for told in range(start, start + 8):
+                pl.semaphore_signal(passed, inc=1, device_id=(told, dp), device_id_type=MESH)
+
     gap = jnp.where(pair < TURN, 2 * TURN - 1 - 2 * pair, 2 * pair + 1 - 2 * TURN)
     lag = jnp.minimum(gap * LAG // 4, MICRO)
     deep_lag = jnp.where(deep_first, 0, lag)
@@ -315,19 +348,47 @@
         turn(run_deep, deep_lag)
         turn(run_wide, wide_lag)
 
-        @pl.when(jnp.logical_and(early, t == MICRO - 1))
-        def _():
-            gather_c()
-
-    def take_x(k):
-        for index in range(7):
-            x_link(k, index, x_win.at[dp, k]).wait_recv()
-
-    each(take_x)
+        @pl.when(t == MICRO - 1)
+        def _():
+            tell(8, 0)
+            tell(23, 24)
+
+            @pl.when(plane == 0)
+            def _():
+                pl.semaphore_wait(passed, 1)
+                send_own_x()
+
+            @pl.when(early)
+            def _():
+                pl.semaphore_wait(passed, 1)
+                gather_sides()
+                gather_rest()
+
+        @pl.when(t == MICRO + TELL)
+        def _():
+            tell(7, 8)
+            tell(24, 16)
+
+    @pl.when(middle)
+    def _():
+        each(pass_close)
+        pl.semaphore_wait(passed, 1)
+        each(lambda k: c_side(k).start())
+
+    @pl.when(plane > 0)
+    def _():
+        send_own_x()
 
     @pl.when(jnp.logical_not(early))
     def _():
-        gather_c()
+        gather_sides()
+
+    @pl.when(plane == 0)
+    def _():
+        gather_rest()
+
+    for index in range(7):
+        x_link(index, x_win.at[dp]).wait_recv()
 
     for g in range(8):
         x_t[:, g * GROUP:(g + 1) * GROUP] = x_win[g].reshape(GROUP, WIN).T
@@ -372,6 +433,10 @@
         )
         one.start()
         shares.append(one)
+
+    @pl.when(middle)
+    def _():
+        gather_rest()
 
     left = unfold(a_inv[...])
 
@@ -393,9 +458,6 @@
 
     def close_sends(k):
         to_mate(k).wait_send()
-        for index in range(7):
-            x_link(k, index, x_win.at[dp, k]).wait_send()
-
         @pl.when(jnp.logical_not(at_end))
         def _():
             for n in range(len(CUTS)):
@@ -406,6 +468,8 @@
         sent(c_ring(k, other_hi, 4))
 
     each(close_sends)
+    for index in range(7):
+        x_link(index, x_win.at[dp]).wait_send()
 
 
 def local(inputs, cotangent, weight, a_inv, g_inv):
@@ -432,8 +496,8 @@
             pltpu.VMEM((8, ROWS, 128), BF16),
             dma((14,)), dma((14,)),
             dma((MICRO, len(CUTS))), dma((MICRO, len(CUTS))), dma((MICRO,)), dma((MICRO,)),
-            dma((MICRO, 7)), dma((MICRO, 7)), dma((MICRO, 9)), dma((MICRO, 9)),
-            dma((7,)), dma((7,)),
+            dma((7,)), dma((7,)), dma((MICRO, 9)), dma((MICRO, 9)),
+            dma((7,)), dma((7,)), pltpu.SemaphoreType.REGULAR,
         ],
         compiler_params=pltpu.CompilerParams(
             collective_id=0, has_side_effects=True, vmem_limit_bytes=56 << 20

time: 348 us -> 330 us (0.948); the launches traced: 348 us -> 325 us
  Pallas kernels: 342 us -> 318 us
    pallas_call x1, Pallas kernels: 342 us -> 318 us  [local(): pl.pallas_call(kernel, out_shape=(jax.ShapeDtypeStruct((ROWS, WD), BF16),...]
where the time goes in v3:
time: 330 us; the launch traced here: 325 us
  Pallas kernels  318 us (96%)
  local copies, waits for them, and re-layouts  5.65 us (2%)
    pallas_call x1, Pallas kernels, local(): pl.pallas_call(kernel, out_shape=(jax.ShapeDtypeStruct((ROWS, WD), BF16),...  318 us

profile of v3, /device:TPU:1, one launch (start us, length us, event | category | flops | bytes accessed | tf_op | source)
XLA Modules:
  0.0 324.5 jit_solution(2025199449166675073)
XLA Ops:
  0.6 318.2 %kfac.1 = (bf16[320,2560]{1,0:T(8,128)(2,1)}, f32[2560,64]{1,0:T(8,128)}, f32[2560,64]{1,0:T(8,128)}) custom-call(bf16[4,32,2560]{2,1,0:T(8,128)(2,1)} %x_in.1, bf16[4,32,2560]{2,1,0:T(8,128)(2,1)} %c_in.1, bf16[320,2560]{1,0:T(8,128)(2,1)} %bitcast.9, bf16[320,64]{1,0:T(8,128)(2,1)} %bitcast.11, bf16[2560,64]{1,0:T(8,128)(2,1)} %bitcast.10), custom_call_target="tpu_custom_call" | custom-call | flops 6442450944 | bytes 8388608 | tf_op jit(solution)/shard_map/kfac/pallas_call | solution.py:479
  318.9 0.0 copy-start.1
  318.9 2.8 copy.11
  321.7 0.0 copy-done.1
  321.7 0.0 copy-start
  321.7 1.1 copy.12
  322.8 0.7 copy-done
  323.5 1.1 copy.13
Async XLA Ops:
  318.9 2.8 copy-start.1
  321.7 1.8 copy-start

commit v4 on v3

--- a/solution.py
+++ b/solution.py
@@ -40,7 +40,7 @@
     x_in, c_in, w_in, a_inv, g_inv,
     w_out, a_out, g_out,
     deep_w, wide_w, deep_in, wide_in, deep_out, wide_out, acc,
-    x_win, c_all, x_t, fac,
+    x_win, c_all, x_t, fac, left_w, right_w,
     gat_send, gat_recv, deep_send, deep_recv, wide_send, wide_recv,
     x_send, x_recv, c_send, c_recv, fac_send, fac_recv, passed,
 ):
@@ -125,6 +125,40 @@
         for slot in range(4):
             links(slot).wait_send()
 
+    def select(height, width):
+        return (
+            lax.rem(lax.broadcasted_iota(jnp.int32, (height, width), 0), 64)
+            == lax.broadcasted_iota(jnp.int32, (height, width), 1)
+        )
+
+    def same_block(size):
+        return (
+            lax.broadcasted_iota(jnp.int32, (size, size), 0) // 64
+            == lax.broadcasted_iota(jnp.int32, (size, size), 1) // 64
+        )
+
+    def fold(gram, width=64):
+        size = gram.shape[0]
+        kept = jnp.where(same_block(size), gram, 0.0)
+        return jnp.dot(
+            kept, select(size, width).astype(F32), precision=lax.Precision.HIGHEST,
+            preferred_element_type=F32,
+        )
+
+    def unfold(blocks):
+        size = blocks.shape[0]
+        tiled = lax.dot_general(
+            blocks, select(size, 64).astype(BF16), (((1,), (1,)), ((), ())), preferred_element_type=F32
+        )
+        return jnp.where(same_block(size), tiled, 0.0).astype(BF16)
+
+    def lay_out_inverses():
+        left_w[...] = unfold(a_inv[...])
+
+        @pl.loop(0, 10)
+        def _(n):
+            right_w[n] = unfold(g_inv[rows(n * 256, 256), :])
+
     def gather_weight(full, flipped):
         def block(group, low, size):
             def view(owner, part=None):
@@ -154,6 +188,7 @@
         close(0).start()
         close(1).start()
         full[rows(dp * ROWS, ROWS), :] = w_in[...]
+        lay_out_inverses()
         for part in range(2):
             view = block(other_hi, part * half, half)
             rings.append(links_of(view, view(y), 4 + 4 * part))
@@ -394,33 +429,6 @@
         x_t[:, g * GROUP:(g + 1) * GROUP] = x_win[g].reshape(GROUP, WIN).T
     own_rows = rows(64 * lax.rem(y, 2), ROWS)
 
-    def select(height, width):
-        return (
-            lax.rem(lax.broadcasted_iota(jnp.int32, (height, width), 0), 64)
-            == lax.broadcasted_iota(jnp.int32, (height, width), 1)
-        )
-
-    def same_block(size):
-        return (
-            lax.broadcasted_iota(jnp.int32, (size, size), 0) // 64
-            == lax.broadcasted_iota(jnp.int32, (size, size), 1) // 64
-        )
-
-    def fold(gram, width=64):
-        size = gram.shape[0]
-        kept = jnp.where(same_block(size), gram, 0.0)
-        return jnp.dot(
-            kept, select(size, width).astype(F32), precision=lax.Precision.HIGHEST,
-            preferred_element_type=F32,
-        )
-
-    def unfold(blocks):
-        size = blocks.shape[0]
-        tiled = lax.dot_general(
-            blocks, select(size, 64).astype(BF16), (((1,), (1,)), ((), ())), preferred_element_type=F32
-        )
-        return jnp.where(same_block(size), tiled, 0.0).astype(BF16)
-
     def contract(a, b):
         return lax.dot_general(a, b, (((1,), (1,)), ((), ())), preferred_element_type=F32)
 
@@ -438,7 +446,6 @@
     def _():
         gather_rest()
 
-    left = unfold(a_inv[...])
 
     @pl.loop(0, 10)
     def _(n):
@@ -446,9 +453,8 @@
         c_cols = c_all[:, :, :, cols].reshape(TOK, 256)
         g_out[rows(n * 256, 256), :] = fold(jnp.dot(c_cols.T, c_cols, preferred_element_type=F32) / TOK)
         grad = jnp.dot(x_t[own_rows, :], c_cols, preferred_element_type=F32) / TOK
-        halfway = jnp.dot(left, grad.astype(BF16), preferred_element_type=F32).astype(BF16)
-        right = unfold(g_inv[rows(n * 256, 256), :])
-        step = jnp.dot(halfway, right, preferred_element_type=F32)
+        halfway = jnp.dot(left_w[...], grad.astype(BF16), preferred_element_type=F32).astype(BF16)
+        step = jnp.dot(halfway, right_w[n], preferred_element_type=F32)
         w_out[:, cols] = (w_in[:, cols].astype(F32) - step).astype(BF16)
 
     for one in shares:
@@ -494,6 +500,8 @@
             pltpu.VMEM((8, MICRO, M, WD), BF16),
             pltpu.VMEM((WIN, TOK), BF16),
             pltpu.VMEM((8, ROWS, 128), BF16),
+            pltpu.VMEM((ROWS, ROWS), BF16),
+            pltpu.VMEM((10, 256, 256), BF16),
             dma((14,)), dma((14,)),
             dma((MICRO, len(CUTS))), dma((MICRO, len(CUTS))), dma((MICRO,)), dma((MICRO,)),
             dma((7,)), dma((7,)), dma((MICRO, 9)), dma((MICRO, 9)),

time: 330 us -> 329 us (level)
  no operation moved by 1% of the time
where the time goes in v4:
time: 329 us; the launch traced here: 325 us
  Pallas kernels  318 us (97%)
  local copies, waits for them, and re-layouts  5.65 us (2%)
    pallas_call x1, Pallas kernels, local(): pl.pallas_call(kernel, out_shape=(jax.ShapeDtypeStruct((ROWS, WD), BF16),...  318 us

profile of v4, /device:TPU:1, one launch (start us, length us, event | category | flops | bytes accessed | tf_op | source)
XLA Modules:
  0.0 324.5 jit_solution(16815317811900896720)
XLA Ops:
  0.6 318.2 %kfac.1 = (bf16[320,2560]{1,0:T(8,128)(2,1)}, f32[2560,64]{1,0:T(8,128)}, f32[2560,64]{1,0:T(8,128)}) custom-call(bf16[4,32,2560]{2,1,0:T(8,128)(2,1)} %x_in.1, bf16[4,32,2560]{2,1,0:T(8,128)(2,1)} %c_in.1, bf16[320,2560]{1,0:T(8,128)(2,1)} %bitcast.9, bf16[320,64]{1,0:T(8,128)(2,1)} %bitcast.11, bf16[2560,64]{1,0:T(8,128)(2,1)} %bitcast.10), custom_call_target="tpu_custom_call" | custom-call | flops 6442450944 | bytes 8388608 | tf_op jit(solution)/shard_map/kfac/pallas_call | solution.py:485
  318.9 0.0 copy-start.1
  318.9 2.8 copy.11
  321.7 0.0 copy-done.1
  321.7 0.0 copy-start
  321.7 1.1 copy.12
  322.8 0.7 copy-done
  323.5 1.1 copy.13
Async XLA Ops:
  318.9 2.8 copy-start.1
  321.7 1.8 copy-start
